TPU v7x, 256 devices: a whole 4x4x8 slice. The times are simulated.
256 devices in a mesh: row: 8 (over y, z_hi), col: 32 (over x, z_lo, core).
Axes of the slice: x: 4, y: 4, z: 8 (z_hi: 2, z_lo: 4; z = z_hi * 4 + z_lo), core: 2. Of those that a mesh axis runs over, the one named last changes fastest.
Arguments:
- a_values: bfloat16 [2, 12288, 4096], P(None, 'row', 'col'), may hold values from -0.44140625 to 0.44140625
- a_pattern: int32 [2, 96, 32], P(None, 'row', 'col'), may hold values 0 or 1
- c_mask: int32 [96, 96], P('row', 'col'), may hold values 0 or 1
Outputs:
- scores: float32 [12288, 12288], P('row', 'col')
All inputs are finite; a program needn't handle non-finite values. No bound on the sum of `a_pattern` or of `c_mask` on one device may be relied on, other than what follows from the above.
Results may differ from a plain program's by a relative error of at most 0.0003.
Values may be sent and summed in bfloat16 or wider, within the bound.
A program may use at most 128 MiB of HBM per device.

v0:
```python
import jax
import jax.numpy as jnp
from jax import lax
from jax.sharding import PartitionSpec as P

TILE = 128
SECTIONS = 2


def spread_tiles(pattern):
    grown = jnp.repeat(pattern, TILE, axis=-2)
    return jnp.repeat(grown, TILE, axis=-1)


def product_nt(left, right):
    return lax.dot_general(
        left, right, (((1,), (1,)), ((), ())), preferred_element_type=jnp.float32
    )


def shards(a_values, a_pattern, c_mask):
    live_tiles = a_values * spread_tiles(a_pattern).astype(jnp.bfloat16)
    row_count = live_tiles.shape[1]
    col_width = c_mask.shape[1] * TILE
    total = jnp.zeros((row_count, col_width), jnp.float32)
    for section in range(SECTIONS):
        local_panel = live_tiles[section]
        all_pages = lax.all_gather(local_panel, "row", axis=0, tiled=True)
        column_block = lax.all_to_all(all_pages, "col", split_axis=0, concat_axis=1, tiled=True)
        total = total + product_nt(
            lax.all_gather(local_panel, "col", axis=1, tiled=True), column_block
        )
    return total * spread_tiles(c_mask).astype(jnp.float32)


def solution(mesh):
    return jax.shard_map(
        shards,
        mesh=mesh,
        in_specs=(P(None, "row", "col"), P(None, "row", "col"), P("row", "col")),
        out_specs=P("row", "col"),
        check_vma=False,
    )
```

profile of v0, /device:TPU:97, one launch (start us, length us, event | category | flops | bytes accessed | tf_op | source)
XLA Modules:
  0.0 493.8 jit_solution(13141279547738618645)
XLA Ops:
  6.5 0.0 all-gather.15.cloned.1.call-start
  6.5 0.7 convert_element_type.22
  7.2 0.1 broadcast_bitcast_fusion.1
  7.3 1.6 broadcast_multiply_fusion
  8.9 1.0 fusion.10
  9.9 0.0 all-gather.15.cloned.1.call-update
  9.9 0.0 all-gather.11.cloned.1.call-start
  10.0 0.7 all-gather.11.cloned.1.call-update
  10.7 0.0 all-gather.13.cloned.1.call-start
  10.7 0.7 all-gather.13.cloned.1.call-update
  11.4 0.0 all-gather.9.cloned.1.call-start
  11.4 0.5 all-gather.9.cloned.1.call-update
  12.0 87.4 %all-gather.15.cloned.1.call-done = bf16[1,12288,128]{2,1,0:T(8,128)(2,1)} async-done(((bf16[1,1536,128]{2,1,0:T(8,128)(2,1)}), bf16[1,12288,128]{2,1,0:T(8,128)(2,1)}) %all-gather.15.cloned.1.call-update) | async-done | bytes 3145744 | tf_op jit(solution)/shard_map/all_gather | solution.py:28
  99.4 9.5 %all-to-all-start.1 = ((bf16[32,384,128]{2,1,0:T(8,128)(2,1)}), bf16[32,384,128]{2,1,0:T(8,128)(2,1)S(1)}, u32[]{:S(2)}, u32[]{:S(2)}) async-start(bf16[32,384,128]{2,1,0:T(8,128)(2,1)} %bitcast.37), calls=%async_computation.1 | async-start | bytes 6291456 | tf_op jit(solution)/shard_map/all_to_all | solution.py:29
  108.9 104.7 %all-gather.11.cloned.1.call-done = bf16[1,12288,128]{2,1,0:T(8,128)(2,1)} async-done(((bf16[1,1536,128]{2,1,0:T(8,128)(2,1)}), bf16[1,12288,128]{2,1,0:T(8,128)(2,1)}) %all-gather.11.cloned.1.call-update) | async-done | bytes 3145744 | tf_op jit(solution)/shard_map/all_gather | solution.py:28
  213.6 6.6 %all-to-all-done.1 = bf16[32,384,128]{2,1,0:T(8,128)(2,1)S(1)} async-done(((bf16[32,384,128]{2,1,0:T(8,128)(2,1)}), bf16[32,384,128]{2,1,0:T(8,128)(2,1)S(1)}, u32[]{:S(2)}, u32[]{:S(2)}) %all-to-all-start.1) | async-done | bytes 3145760 | tf_op jit(solution)/shard_map/all_to_all | solution.py:29
  220.2 0.0 copy-start
  220.2 8.6 %all-to-all-start = ((bf16[32,384,128]{2,1,0:T(8,128)(2,1)}), bf16[32,384,128]{2,1,0:T(8,128)(2,1)}, u32[]{:S(2)}, u32[]{:S(2)}) async-start(bf16[32,384,128]{2,1,0:T(8,128)(2,1)} %bitcast.36), calls=%async_computation | async-start | bytes 6291456 | tf_op jit(solution)/shard_map/all_to_all | solution.py:29
  228.8 0.0 copy-done
  228.9 0.1 broadcast_bitcast_fusion
  228.9 1.7 broadcast_in_dim.12
  230.6 3.1 copy.8
  233.7 2.8 copy.7
  236.5 79.0 %all-to-all-done = bf16[32,384,128]{2,1,0:T(8,128)(2,1)} async-done(((bf16[32,384,128]{2,1,0:T(8,128)(2,1)}), bf16[32,384,128]{2,1,0:T(8,128)(2,1)}, u32[]{:S(2)}, u32[]{:S(2)}) %all-to-all-start) | async-done | bytes 3145760 | tf_op jit(solution)/shard_map/all_to_all | solution.py:29
  315.5 3.5 copy.6
  318.9 49.2 %all-gather.13.cloned.1.call-done = bf16[1,1536,4096]{2,1,0:T(8,128)(2,1)} async-done(((bf16[1,1536,128]{2,1,0:T(8,128)(2,1)}), bf16[1,1536,4096]{2,1,0:T(8,128)(2,1)}) %all-gather.13.cloned.1.call-update) | async-done | bytes 12582928 | tf_op jit(solution)/shard_map/all_gather | solution.py:31
  368.1 11.6 %fusion = f32[1536,384]{1,0:T(8,128)} fusion(bf16[384,4096]{0,1:T(8,128)(2,1)} %bitcast.39, bf16[1,1536,4096]{2,1,0:T(8,128)(2,1)} %all-gather.13.cloned.1.call-done), kind=kOutput, calls=%fused_computation | convolution fusion | flops 4831838208 | bytes 18087936 | tf_op jit(solution)/shard_map/dot_general | solution.py:16
  379.8 96.2 %all-gather.9.cloned.1.call-done = bf16[1,1536,4096]{2,1,0:T(8,128)(2,1)} async-done(((bf16[1,1536,128]{2,1,0:T(8,128)(2,1)}), bf16[1,1536,4096]{2,1,0:T(8,128)(2,1)}) %all-gather.9.cloned.1.call-update) | async-done | bytes 12582928 | tf_op jit(solution)/shard_map/all_gather | solution.py:31
  476.0 11.3 %fusion.7 = f32[1536,384]{1,0:T(8,128)} fusion(f32[1536,384]{1,0:T(8,128)} %copy.8, f32[1536,384]{1,0:T(8,128)} %fusion, bf16[384,4096]{0,1:T(8,128)(2,1)S(1)} %bitcast.38, bf16[1,1536,4096]{2,1,0:T(8,128)(2,1)} %all-gather.9.cloned.1.call-done), kind=kOutput, calls=%fused_computation.5 | convolution fusion | flops 4833017856 | bytes 22806528 | tf_op jit(solution)/shard_map/dot_general | solution.py:16
  (4 shorter events, 0.0 us)
Async XLA Ops:
  6.5 92.8 %all-gather.15.cloned.1.call-start = ((), (), s32[]{:S(2)}) async-start(), calls=%async_computation.5 | async-start | bytes 3538944 | tf_op jit(solution)/shard_map/all_gather | solution.py:28
  9.9 203.7 %all-gather.11.cloned.1.call-start = ((), (), s32[]{:S(2)}) async-start(), calls=%async_computation.3 | async-start | bytes 3538944 | tf_op jit(solution)/shard_map/all_gather | solution.py:28
  10.7 357.5 %all-gather.13.cloned.1.call-start = ((), (), s32[]{:S(2)}) async-start(), calls=%async_computation.4 | async-start | bytes 12976128 | tf_op jit(solution)/shard_map/all_gather | solution.py:31
  11.4 464.6 %all-gather.9.cloned.1.call-start = ((), (), s32[]{:S(2)}) async-start(), calls=%async_computation.2 | async-start | bytes 12976128 | tf_op jit(solution)/shard_map/all_gather | solution.py:31
  99.4 120.8 %all-to-all-start.1 = ((bf16[32,384,128]{2,1,0:T(8,128)(2,1)}), bf16[32,384,128]{2,1,0:T(8,128)(2,1)S(1)}, u32[]{:S(2)}, u32[]{:S(2)}) async-start(bf16[32,384,128]{2,1,0:T(8,128)(2,1)} %bitcast.37), calls=%async_computation.1 | async-start | bytes 6291456 | tf_op jit(solution)/shard_map/all_to_all | solution.py:29
  220.2 8.7 %copy-start = (s32[12,3]{0,1:T(4,128)S(1)}, s32[12,3]{0,1:T(4,128)}, u32[]{:S(2)}) copy-start(s32[12,3]{0,1:T(4,128)} %param.5) | copy-start | bytes 436
  220.2 95.3 %all-to-all-start = ((bf16[32,384,128]{2,1,0:T(8,128)(2,1)}), bf16[32,384,128]{2,1,0:T(8,128)(2,1)}, u32[]{:S(2)}, u32[]{:S(2)}) async-start(bf16[32,384,128]{2,1,0:T(8,128)(2,1)} %bitcast.36), calls=%async_computation | async-start | bytes 6291456 | tf_op jit(solution)/shard_map/all_to_all | solution.py:29
Sparse Core Ops, SparseCore 0:
  10.0 89.3 all-gather.14
  102.0 111.5 all-gather.10
  215.4 152.7 all-gather.12
  369.8 106.1 all-gather.8
where the time goes:
time: 499 us; the launch traced here: 494 us
  waiting for transfers between devices  425 us (85%)
  matrix products  23 us (5%)
  starting transfers between devices  18.3 us (4%)
  between operations  13.2 us (3%)
  local copies, waits for them, and re-layouts  12.2 us (2%)
    all_gather x2, waiting for transfers between devices, shards(): all_pages = lax.all_gather(local_panel, 'row', axis=0, tiled=True)  192 us
    all_gather x2, waiting for transfers between devices, shards(): lax.all_gather(local_panel, 'col', axis=1, tiled=True)  145 us
    all_to_all x2, waiting for transfers between devices, shards(): lax.all_to_all(all_pages, 'col', split_axis=0, concat_axis=1, tiled=True)  85.5 us
    dot_general x2, matrix products, product_nt(): lax.dot_general(left, right, (((1,), (1,)), ((), ())), preferred_element_...  23 us
    all_to_all x2, starting transfers between devices, shards(): lax.all_to_all(all_pages, 'col', split_axis=0, concat_axis=1, tiled=True)  18.2 us
  transfers between devices with their start and end apart: 6, of which 6 were waited for; matrix products, arithmetic and copies ran while one was open for 5% of the time, Pallas kernels for 0%

commit v1 on v0

v1 whole, which is shorter than its diff:
```python
import functools

import jax
import jax.numpy as jnp
from jax import lax
from jax.experimental import pallas as pl
from jax.experimental.pallas import tpu as pltpu
from jax.sharding import PartitionSpec as P

TILE = 128
SECTIONS = 2
MESH = pl.DeviceIdType.MESH
LAST_TICK = 28


def kernel(rows, a_ref, pat_ref, mask_ref, out_ref, row, col, acc, got,
           zs, zr, xs, xr, ys, cr, cs, es, er):
    half, quarter = rows // 2, rows // 4
    width = half // 2
    tiles = rows // TILE

    row_id, col_id = lax.axis_index("row"), lax.axis_index("col")
    y, h = lax.div(row_id, 2), lax.rem(row_id, 2)
    x, zl, core = lax.div(col_id, 8), lax.rem(lax.div(col_id, 2), 4), lax.rem(col_id, 2)
    a, b = lax.div(zl, 2), lax.rem(zl, 2)
    x_up, x_down, x_far = lax.rem(x + 1, 4), lax.rem(x + 3, 4), lax.rem(x + 2, 4)
    ring = lax.rem(y - x + 4, 4)
    straight = h == a

    def device(x=x, y=y, h=h, zl=zl, core=core):
        return (y * 2 + h, x * 8 + zl * 2 + core)

    dev_x_up, dev_x_down = device(x=x_up), device(x=x_down)
    dev_y_up, dev_y_down = device(y=lax.rem(y + 1, 4)), device(y=lax.rem(y + 3, 4))
    dev_over, dev_core = device(h=1 - h), device(core=1 - core)
    z_peers = [lax.rem(zl + d, 4) for d in (1, 2, 3)]
    partners = [dev_x_up, dev_x_down, dev_y_up, dev_y_down, dev_over, dev_core]
    partners += [device(zl=z) for z in z_peers]

    barrier = pltpu.get_barrier_semaphore()
    for partner in partners:
        pl.semaphore_signal(barrier, inc=1, device_id=partner, device_id_type=MESH)

    own = x * 4 + zl

    def mask_tile(t, _):
        place = pl.ds(pl.multiple_of(t * TILE, TILE), TILE)
        for section in range(SECTIONS):
            keep = pat_ref[section, t, 0].astype(jnp.float32)
            tile = a_ref[section, place, :].astype(jnp.float32) * keep
            row[own, section, place, :] = tile.astype(jnp.bfloat16)
        return 0

    lax.fori_loop(0, tiles, mask_tile, 0)
    acc[...] = jnp.zeros_like(acc)
    pl.semaphore_wait(barrier, len(partners))

    def send(src, dst, send_sem, recv_sem, target):
        return pltpu.make_async_remote_copy(
            src_ref=src, dst_ref=dst, send_sem=send_sem, recv_sem=recv_sem,
            device_id=target, device_id_type=MESH)

    def row_half(s, g):
        return row.at[s, :, pl.ds(pl.multiple_of(g * half, half), half), :]

    def row_part(s, g, q):
        return row.at[s, :, pl.ds(pl.multiple_of(g * half + q * quarter, quarter), quarter), :]

    def col_part(s, q):
        return col.at[s, :, pl.ds(pl.multiple_of(q * quarter, quarter), quarter), :]

    def z_of(k):
        return 2 * lax.rem(a + lax.div(k, 2), 2) + lax.rem(b + lax.rem(k, 2), 2)

    def half_of(i):
        return lax.rem(b + lax.div(i, 4), 2)

    def wait_row(s, g, q):
        ref = row_part(s, g, q)
        send(ref, ref, xs.at[0, 0, 0], xr.at[s, g, q], dev_x_up).wait_recv()

    def wait_col(s, q):
        ref = col_part(s, q)
        send(ref, ref, xs.at[0, 0, 0], cr.at[s, q], dev_y_up).wait_recv()

    def send_item(i):
        s, g = x * 4 + z_of(lax.rem(i, 4)), half_of(i)
        for n, (way, q, target) in enumerate(
                ((0, 0, dev_x_up), (1, 1, dev_x_down), (0, 1, dev_x_up), (1, 0, dev_x_down))):
            ref = row_part(s, g, q)
            send(ref, ref, xs.at[way, i, n // 2], xr.at[s, g, q], target).start()

    send_item(jnp.int32(0))
    for late in range(2):
        for n, z in enumerate(z_peers):
            g = lax.rem(z + late, 2)
            ref = row_half(own, g)
            send(ref, ref, zs.at[late, n], zr.at[zl, g], device(zl=z)).start()

    def slice_of(n):
        o = lax.rem(n, 4)
        step = jnp.where(o == 0, 0, jnp.where(o == 1, 3, jnp.where(o == 2, 1, 2)))
        return lax.rem(x + step, 4) * 4 + z_of(lax.div(n, 4))

    def crossing(j, r, second):
        odd = lax.rem(r, 2)
        n = 4 * j + jnp.where(r == 0, 3, odd) + second * odd
        q = jnp.where(odd == 1, lax.div(r, 2), second)
        return slice_of(n), q

    def accumulate(group, f):
        g = lax.rem(b + f, 2)
        block = min(256, half)

        def one(t, _):
            place = pl.ds(pl.multiple_of(g * half + t * block, block), block)
            for side in range(2):
                total = acc[side, place, :]
                for o in range(4):
                    s = slice_of(group * 4 + o)
                    left = jnp.concatenate([row[s, 0, place, :], row[s, 1, place, :]], axis=1)
                    span = pl.ds(side * width, width)
                    right = jnp.concatenate([col[s, 0, span, :], col[s, 1, span, :]], axis=1)
                    total = total + lax.dot_general(
                        left, right, (((1,), (1,)), ((), ())), preferred_element_type=jnp.float32)
                acc[side, place, :] = total
            return 0

        lax.fori_loop(0, half // block, one, 0)

    def tick(m, _):
        i, sub = lax.div(m, 3), lax.rem(m, 3)

        @pl.when((sub == 0) & (i >= 1) & (i <= 8))
        def _():
            z, g = z_of(lax.rem(i - 1, 4)), half_of(i - 1)
            wait_row(x_down * 4 + z, g, 1)
            wait_row(x_up * 4 + z, g, 0)
            wait_row(x_far * 4 + z, g, 0)
            wait_row(x_far * 4 + z, g, 1)

        @pl.when((sub == 1) & (i < 8))
        def _():
            z, g = z_of(lax.rem(i, 4)), half_of(i)
            for way, q, source, target in ((0, 0, x_down, dev_x_up), (1, 1, x_up, dev_x_down)):
                s = source * 4 + z
                wait_row(s, g, q)
                ref = row_part(s, g, q)
                send(ref, ref, xs.at[way, i, 2], xr.at[s, g, q], target).start()

        @pl.when((sub == 2) & (i < 7))
        def _():
            @pl.when(lax.rem(i + 1, 4) != 0)
            def _():
                z, g = z_of(lax.rem(i + 1, 4)), half_of(i + 1)
                ref = row_half(x * 4 + z, g)
                send(ref, ref, xs.at[0, 0, 0], zr.at[z, g], dev_x_up).wait_recv()

            send_item(i + 1)

        @pl.when(straight)
        def _():
            @pl.when((ring == 0) & (m >= 2) & (m < 18))
            def _():
                s = slice_of(m - 2)
                col[s] = row[s, :, pl.ds(pl.multiple_of(b * half, half), half), :]
                for q, target in ((0, dev_y_up), (1, dev_y_down)):
                    send(row_part(s, b, q), col_part(s, q), ys.at[q, m - 2, 0], cr.at[s, q], target).start()

            for q, target in ((0, dev_y_up), (1, dev_y_down)):
                hops = ring if q == 0 else 4 - ring
                n = m - 2 - 2 * hops

                @pl.when((ring != 0) & (n >= 0) & (n < 16))
                def _():
                    s = slice_of(n)
                    wait_col(s, q)

                    @pl.when(hops < 3)
                    def _():
                        ref = col_part(s, q)
                        send(ref, ref, ys.at[q, n, 0], cr.at[s, q], target).start()

            @pl.when((m >= 6) & (m < 22) & (lax.rem(m, 4) == 2))
            def _():
                j = lax.div(m - 6, 4)
                for second in range(2):
                    s, q = crossing(j, ring, second)
                    ref = col_part(s, q)
                    send(ref, ref, cs.at[j, second], cr.at[s, q], dev_over).start()

            @pl.when((m >= 12) & (m < 28) & (lax.rem(m, 4) == 0))
            def _():
                accumulate(lax.div(m - 12, 4), 0)

            @pl.when((m >= 15) & (m < 27) & (sub == 0))
            def _():
                accumulate(lax.div(m - 15, 3), 1)

        @pl.when(jnp.logical_not(straight))
        def _():
            phase = lax.rem(m + 2, 4)
            r_down, r_up, r_far = lax.rem(ring + 3, 4), lax.rem(ring + 1, 4), lax.rem(ring + 2, 4)

            @pl.when((phase == 0) & (m >= 14))
            def _():
                j = lax.div(m - 14, 4)
                for r, second in ((r_down, 1), (r_up, 0), (r_far, 0), (r_far, 1)):
                    wait_col(*crossing(j, r, second))

            @pl.when((phase == 0) & (m >= 10) & (m < 26))
            def _():
                j = lax.div(m - 10, 4)
                parts = [crossing(j, ring, second) for second in range(2)]
                for s, q in parts:
                    wait_col(s, q)
                for n, (way, second, target) in enumerate(
                        ((0, 0, dev_y_up), (1, 1, dev_y_down), (0, 1, dev_y_up), (1, 0, dev_y_down))):
                    s, q = parts[second]
                    ref = col_part(s, q)
                    send(ref, ref, ys.at[way, j, n // 2], cr.at[s, q], target).start()

            @pl.when((phase == 2) & (m >= 12) & (m < 28))
            def _():
                j = lax.div(m - 12, 4)
                for way, r, target in ((0, r_down, dev_y_up), (1, r_up, dev_y_down)):
                    s, q = crossing(j, r, way)
                    wait_col(s, q)
                    ref = col_part(s, q)
                    send(ref, ref, ys.at[way, j, 2], cr.at[s, q], target).start()

            @pl.when((phase == 1) & (m >= 15))
            def _():
                accumulate(lax.div(m - 15, 4), 0)
                accumulate(lax.div(m - 15, 4), 1)

        return 0

    lax.fori_loop(0, LAST_TICK, tick, 0)

    def trade(f):
        g = lax.rem(b + f, 2)
        place = pl.ds(pl.multiple_of(g * half, half), half)
        return send(acc.at[1 - core, place, :], got.at[place, :], es.at[f], er.at[f], dev_core)

    trades = [trade(0), trade(1)]
    for one in trades:
        one.start()
    for f, one in enumerate(trades):
        one.wait_recv()
        first = lax.rem(b + f, 2) * (tiles // 2)

        def finish(t, _):
            tile_row = first + t
            place = pl.ds(pl.multiple_of(tile_row * TILE, TILE), TILE)
            for c in range(width // TILE):
                span = pl.ds(c * TILE, TILE)
                keep = mask_ref[tile_row, c].astype(jnp.float32)
                out_ref[place, span] = (acc[core, place, span] + got[place, span]) * keep
            return 0

        lax.fori_loop(0, tiles // 2, finish, 0)

    part = row_part(0, 0, 0)
    whole = row_half(0, 0)
    for one in trades:
        one.wait_send()
    for late in range(2):
        for n in range(3):
            send(whole, whole, zs.at[late, n], zr.at[0, 0], dev_x_up).wait_send()

    def drain_x(i, _):
        for way in range(2):
            for n in range(3):
                send(part, part, xs.at[way, i, n], xr.at[0, 0, 0], dev_x_up).wait_send()
        return 0

    lax.fori_loop(0, 8, drain_x, 0)

    @pl.when(straight)
    def _():
        def drain(n, _):
            for q in range(2):
                hops = ring if q == 0 else lax.rem(4 - ring, 4)

                @pl.when(hops < 3)
                def _():
                    send(part, part, ys.at[q, n, 0], xr.at[0, 0, 0], dev_x_up).wait_send()
            return 0

        lax.fori_loop(0, 16, drain, 0)

        def drain_over(j, _):
            for second in range(2):
                send(part, part, cs.at[j, second], xr.at[0, 0, 0], dev_x_up).wait_send()
            return 0

        lax.fori_loop(0, 4, drain_over, 0)

    @pl.when(jnp.logical_not(straight))
    def _():
        def drain(j, _):
            for way in range(2):
                for n in range(3):
                    send(part, part, ys.at[way, j, n], xr.at[0, 0, 0], dev_x_up).wait_send()
            return 0

        lax.fori_loop(0, 4, drain, 0)


def shards(a_values, a_pattern, c_mask):
    rows, depth = a_values.shape[1], a_values.shape[2]
    out_width = c_mask.shape[1] * TILE
    half = rows // 2
    vmem = pl.BlockSpec(memory_space=pltpu.VMEM)
    smem = pl.BlockSpec(memory_space=pltpu.SMEM)
    dma = pltpu.SemaphoreType.DMA
    return pl.pallas_call(
        functools.partial(kernel, rows),
        out_shape=jax.ShapeDtypeStruct((rows, out_width), jnp.float32),
        in_specs=[vmem, smem, smem],
        out_specs=vmem,
        scratch_shapes=[
            pltpu.VMEM((16, SECTIONS, rows, depth), jnp.bfloat16),
            pltpu.VMEM((16, SECTIONS, half, depth), jnp.bfloat16),
            pltpu.VMEM((2, rows, out_width), jnp.float32),
            pltpu.VMEM((rows, out_width), jnp.float32),
            dma((2, 3)), dma((4, 2)), dma((2, 8, 3)), dma((16, 2, 2)),
            dma((2, 16, 3)), dma((16, 2)), dma((4, 2)), dma((2,)), dma((2,)),
        ],
        compiler_params=pltpu.CompilerParams(
            collective_id=0, has_side_effects=True, vmem_limit_bytes=48 << 20),
        cost_estimate=pl.CostEstimate(
            flops=2 * rows * half * 16 * SECTIONS * depth, bytes_accessed=4 * rows * out_width, transcendentals=0),
        name="gather_and_multiply",
    )(a_values, a_pattern, c_mask)


def solution(mesh):
    return jax.shard_map(
        shards,
        mesh=mesh,
        in_specs=(P(None, "row", "col"), P(None, "row", "col"), P("row", "col")),
        out_specs=P("row", "col"),
        check_vma=False,
    )
```

time: 499 us -> 209 us (0.42); the launches traced: 494 us -> 209 us
  waiting for transfers between devices: 425 us -> 0 us
  Pallas kernels: 0 us -> 205 us
  matrix products: 23 us -> 0 us
  starting transfers between devices: 18.3 us -> 0 us
  between operations: 13.2 us -> 0.01 us
  local copies, waits for them, and re-layouts: 12.2 us -> 4.08 us
    all_gather x4 -> x0, waiting for transfers between devices: 337 us -> none  [the longest x2 192 us: shards(): all_pages = lax.all_gather(local_panel, 'row', axis=0, tiled=True)]
    pallas_call x0 -> x1, Pallas kernels: none -> 205 us  [shards(): pl.pallas_call(functools.partial(kernel, rows), out_shape=jax.ShapeDtypeS...]
    all_to_all x2 -> x0, waiting for transfers between devices: 85.5 us -> none  [shards(): lax.all_to_all(all_pages, 'col', split_axis=0, concat_axis=1, tiled=True)]
    dot_general x2 -> x0, matrix products: 23 us -> none  [product_nt(): lax.dot_general(left, right, (((1,), (1,)), ((), ())), preferred_element_...]
    all_to_all x2 -> x0, starting transfers between devices: 18.2 us -> none  [shards(): lax.all_to_all(all_pages, 'col', split_axis=0, concat_axis=1, tiled=True)]
    all_to_all x2 -> x0, local copies, waits for them, and re-layouts: 6.28 us -> none  [shards(): lax.all_to_all(all_pages, 'col', split_axis=0, concat_axis=1, tiled=True)]
  transfers between devices with their start and end apart: 6 -> 0, of which waited for: 6 -> 0; matrix products, arithmetic and copies ran while one was open for 5% -> 0% of each run, Pallas kernels for 0% -> 0%
where the time goes in v1:
time: 209 us
  Pallas kernels  205 us (98%)
  local copies, waits for them, and re-layouts  4.08 us (2%)
    pallas_call x1, Pallas kernels, shards(): pl.pallas_call(functools.partial(kernel, rows), out_shape=jax.ShapeDtypeS...  205 us

profile of v1, /device:TPU:97, one launch (start us, length us, event | category | flops | bytes accessed | tf_op | source)
XLA Modules:
  0.0 209.1 jit_solution(697449142186869298)
XLA Ops:
  0.0 0.8 copy.5.mask_ref
  0.8 0.8 copy.4.pat_ref
  1.5 0.0 copy-start
  1.5 1.1 copy-done
  2.7 205.0 %gather_and_multiply.1 = f32[1536,384]{1,0:T(8,128)S(1)} custom-call(bf16[2,1536,128]{2,1,0:T(8,128)(2,1)S(1)} %copy-done, s32[2,12,1]{2,1,0:T(8,128)S(1)} %copy.4.pat_ref, s32[12,3]{1,0:T(8,128)S(1)} %copy.5.mask_ref), custom_call_target="tpu_custom_call" | custom-call | flops 9663676416 | bytes 2359296 | tf_op jit(solution)/shard_map/gather_and_multiply/pallas_call | solution.py:318
  207.6 1.4 copy.7
Async XLA Ops:
  1.5 1.1 copy-start

commit v2 on v1

--- a/solution.py
+++ b/solution.py
@@ -13,8 +13,8 @@
 LAST_TICK = 28
 
 
-def kernel(rows, a_ref, pat_ref, mask_ref, out_ref, row, col, acc, got,
-           zs, zr, xs, xr, ys, cr, cs, es, er):
+def kernel(rows, a_ref, pat_ref, mask_ref, out_ref, row, col, acc, got, relay, transit,
+           zs, zr, xs, xr, ys, cr, cs, rr, tr, es, er):
     half, quarter = rows // 2, rows // 4
     width = half // 2
     tiles = rows // TILE
@@ -32,8 +32,8 @@
 
     dev_x_up, dev_x_down = device(x=x_up), device(x=x_down)
     dev_y_up, dev_y_down = device(y=lax.rem(y + 1, 4)), device(y=lax.rem(y + 3, 4))
-    dev_over, dev_core = device(h=1 - h), device(core=1 - core)
-    z_peers = [lax.rem(zl + d, 4) for d in (1, 2, 3)]
+    dev_over, dev_core = device(h=1 - h, zl=2 * (1 - a) + b), device(core=1 - core)
+    z_peers = [2 * lax.rem(a + k // 2, 2) + lax.rem(b + k % 2, 2) for k in (1, 2, 3)]
     partners = [dev_x_up, dev_x_down, dev_y_up, dev_y_down, dev_over, dev_core]
     partners += [device(zl=z) for z in z_peers]
 
@@ -69,8 +69,8 @@
     def col_part(s, q):
         return col.at[s, :, pl.ds(pl.multiple_of(q * quarter, quarter), quarter), :]
 
-    def z_of(k):
-        return 2 * lax.rem(a + lax.div(k, 2), 2) + lax.rem(b + lax.rem(k, 2), 2)
+    def z_of(k, first=a):
+        return 2 * lax.rem(first + lax.div(k, 2), 2) + lax.rem(b + lax.rem(k, 2), 2)
 
     def half_of(i):
         return lax.rem(b + lax.div(i, 4), 2)
@@ -91,22 +91,22 @@
             send(ref, ref, xs.at[way, i, n // 2], xr.at[s, g, q], target).start()
 
     send_item(jnp.int32(0))
-    for late in range(2):
-        for n, z in enumerate(z_peers):
-            g = lax.rem(z + late, 2)
-            ref = row_half(own, g)
-            send(ref, ref, zs.at[late, n], zr.at[zl, g], device(zl=z)).start()
-
-    def slice_of(n):
+    def send_along_z(late, n):
+        g = lax.rem(z_peers[n] + late, 2)
+        ref = row_half(own, g)
+        send(ref, ref, zs.at[late, n], zr.at[zl, g], device(zl=z_peers[n])).start()
+
+    for n in range(3):
+        send_along_z(0, n)
+
+    def slice_of(n, first=h):
         o = lax.rem(n, 4)
         step = jnp.where(o == 0, 0, jnp.where(o == 1, 3, jnp.where(o == 2, 1, 2)))
-        return lax.rem(x + step, 4) * 4 + z_of(lax.div(n, 4))
-
-    def crossing(j, r, second):
-        odd = lax.rem(r, 2)
-        n = 4 * j + jnp.where(r == 0, 3, odd) + second * odd
-        q = jnp.where(odd == 1, lax.div(r, 2), second)
-        return slice_of(n), q
+        return lax.rem(x + step, 4) * 4 + z_of(lax.div(n, 4), first)
+
+    def crossing(j, r, first=h):
+        o = jnp.where(r == 0, 3, jnp.where(r == 2, 0, lax.div(r + 1, 2)))
+        return slice_of(4 * j + o, first)
 
     def accumulate(group, f):
         g = lax.rem(b + f, 2)
@@ -158,6 +158,11 @@
 
             send_item(i + 1)
 
+        for n in range(3):
+            @pl.when(m == 7 + 3 * n)
+            def _():
+                send_along_z(1, n)
+
         @pl.when(straight)
         def _():
             @pl.when((ring == 0) & (m >= 2) & (m < 18))
@@ -181,14 +186,6 @@
                         ref = col_part(s, q)
                         send(ref, ref, ys.at[q, n, 0], cr.at[s, q], target).start()
 
-            @pl.when((m >= 6) & (m < 22) & (lax.rem(m, 4) == 2))
-            def _():
-                j = lax.div(m - 6, 4)
-                for second in range(2):
-                    s, q = crossing(j, ring, second)
-                    ref = col_part(s, q)
-                    send(ref, ref, cs.at[j, second], cr.at[s, q], dev_over).start()
-
             @pl.when((m >= 12) & (m < 28) & (lax.rem(m, 4) == 0))
             def _():
                 accumulate(lax.div(m - 12, 4), 0)
@@ -202,21 +199,68 @@
             phase = lax.rem(m + 2, 4)
             r_down, r_up, r_far = lax.rem(ring + 3, 4), lax.rem(ring + 1, 4), lax.rem(ring + 2, 4)
 
+            @pl.when((ring == 0) & (m >= 2) & (m < 18))
+            def _():
+                j, o = lax.div(m - 2, 4), lax.rem(m - 2, 4)
+                s = slice_of(m - 2, a)
+                first, second = row_part(s, b, 0), row_part(s, b, 1)
+
+                @pl.when(o == 0)
+                def _():
+                    send(first, transit.at[j], cs.at[j, 0], tr.at[j], dev_y_up).start()
+                    send(second, transit.at[j], cs.at[j, 1], tr.at[j], dev_y_down).start()
+
+                @pl.when(o == 1)
+                def _():
+                    send(first, relay.at[j, 0], cs.at[j, 2], rr.at[j, 0], dev_y_up).start()
+                    send(second, relay.at[j, 1], cs.at[j, 3], rr.at[j, 1], dev_y_up).start()
+
+                @pl.when(o == 2)
+                def _():
+                    send(first, relay.at[j, 0], cs.at[j, 4], rr.at[j, 0], dev_y_down).start()
+                    send(second, relay.at[j, 1], cs.at[j, 5], rr.at[j, 1], dev_y_down).start()
+
+                @pl.when(o == 3)
+                def _():
+                    send(first, col_part(s, 0), cs.at[j, 6], cr.at[s, 0], dev_over).start()
+                    send(second, col_part(s, 1), cs.at[j, 7], cr.at[s, 1], dev_over).start()
+
+            @pl.when((lax.rem(ring, 2) == 1) & (phase == 2) & (m >= 4) & (m < 20))
+            def _():
+                j = lax.div(m - 4, 4)
+                send(transit.at[j], transit.at[j], cs.at[j, 0], tr.at[j], dev_y_up).wait_recv()
+
+                @pl.when(ring == 1)
+                def _():
+                    send(transit.at[j], relay.at[j, 0], cs.at[j, 0], rr.at[j, 0], dev_y_up).start()
+
+                @pl.when(ring == 3)
+                def _():
+                    send(transit.at[j], relay.at[j, 1], cs.at[j, 0], rr.at[j, 1], dev_y_down).start()
+
+            @pl.when((ring != 0) & (phase == 1) & (m >= 7) & (m < 23))
+            def _():
+                j = lax.div(m - 7, 4)
+                s = crossing(j, ring, a)
+                for q in range(2):
+                    ref = relay.at[j, q]
+                    send(ref, ref, cs.at[j, 6 + q], rr.at[j, q], dev_over).wait_recv()
+                    send(ref, col_part(s, q), cs.at[j, 6 + q], cr.at[s, q], dev_over).start()
+
             @pl.when((phase == 0) & (m >= 14))
             def _():
                 j = lax.div(m - 14, 4)
-                for r, second in ((r_down, 1), (r_up, 0), (r_far, 0), (r_far, 1)):
-                    wait_col(*crossing(j, r, second))
+                for r, q in ((r_down, 1), (r_up, 0), (r_far, 0), (r_far, 1)):
+                    wait_col(crossing(j, r), q)
 
             @pl.when((phase == 0) & (m >= 10) & (m < 26))
             def _():
                 j = lax.div(m - 10, 4)
-                parts = [crossing(j, ring, second) for second in range(2)]
-                for s, q in parts:
+                s = crossing(j, ring)
+                for q in range(2):
                     wait_col(s, q)
-                for n, (way, second, target) in enumerate(
+                for n, (way, q, target) in enumerate(
                         ((0, 0, dev_y_up), (1, 1, dev_y_down), (0, 1, dev_y_up), (1, 0, dev_y_down))):
-                    s, q = parts[second]
                     ref = col_part(s, q)
                     send(ref, ref, ys.at[way, j, n // 2], cr.at[s, q], target).start()
 
@@ -224,15 +268,18 @@
             def _():
                 j = lax.div(m - 12, 4)
                 for way, r, target in ((0, r_down, dev_y_up), (1, r_up, dev_y_down)):
-                    s, q = crossing(j, r, way)
-                    wait_col(s, q)
-                    ref = col_part(s, q)
-                    send(ref, ref, ys.at[way, j, 2], cr.at[s, q], target).start()
+                    s = crossing(j, r)
+                    wait_col(s, way)
+                    ref = col_part(s, way)
+                    send(ref, ref, ys.at[way, j, 2], cr.at[s, way], target).start()
 
             @pl.when((phase == 1) & (m >= 15))
             def _():
                 accumulate(lax.div(m - 15, 4), 0)
-                accumulate(lax.div(m - 15, 4), 1)
+
+            @pl.when(m >= 24)
+            def _():
+                accumulate(m - 24, 1)
 
         return 0
 
@@ -290,19 +337,16 @@
 
         lax.fori_loop(0, 16, drain, 0)
 
-        def drain_over(j, _):
-            for second in range(2):
-                send(part, part, cs.at[j, second], xr.at[0, 0, 0], dev_x_up).wait_send()
-            return 0
-
-        lax.fori_loop(0, 4, drain_over, 0)
-
     @pl.when(jnp.logical_not(straight))
     def _():
         def drain(j, _):
             for way in range(2):
                 for n in range(3):
                     send(part, part, ys.at[way, j, n], xr.at[0, 0, 0], dev_x_up).wait_send()
+            for n in range(8):
+                @pl.when((ring == 0) | (n >= 6) | ((n == 0) & (ring != 2)))
+                def _():
+                    send(part, part, cs.at[j, n], xr.at[0, 0, 0], dev_x_up).wait_send()
             return 0
 
         lax.fori_loop(0, 4, drain, 0)
@@ -325,8 +369,10 @@
             pltpu.VMEM((16, SECTIONS, half, depth), jnp.bfloat16),
             pltpu.VMEM((2, rows, out_width), jnp.float32),
             pltpu.VMEM((rows, out_width), jnp.float32),
+            pltpu.VMEM((4, 2, SECTIONS, half // 2, depth), jnp.bfloat16),
+            pltpu.VMEM((4, SECTIONS, half // 2, depth), jnp.bfloat16),
             dma((2, 3)), dma((4, 2)), dma((2, 8, 3)), dma((16, 2, 2)),
-            dma((2, 16, 3)), dma((16, 2)), dma((4, 2)), dma((2,)), dma((2,)),
+            dma((2, 16, 3)), dma((16, 2)), dma((4, 8)), dma((4, 2)), dma((4,)), dma((2,)), dma((2,)),
         ],
         compiler_params=pltpu.CompilerParams(
             collective_id=0, has_side_effects=True, vmem_limit_bytes=48 << 20),

time: 209 us -> 153 us (0.73)
  Pallas kernels: 205 us -> 148 us
    pallas_call x1, Pallas kernels: 205 us -> 148 us  [shards(): pl.pallas_call(functools.partial(kernel, rows), out_shape=jax.ShapeDtypeS...]
where the time goes in v2:
time: 153 us; the launch traced here: 152 us
  Pallas kernels  148 us (97%)
  local copies, waits for them, and re-layouts  4.08 us (3%)
    pallas_call x1, Pallas kernels, shards(): pl.pallas_call(functools.partial(kernel, rows), out_shape=jax.ShapeDtypeS...  148 us
    unnamed x5, local copies, waits for them, and re-layouts  4.08 us

profile of v2, /device:TPU:97, one launch (start us, length us, event | category | flops | bytes accessed | tf_op | source)
XLA Modules:
  0.0 151.6 jit_solution(3296694553694104845)
XLA Ops:
  0.0 0.8 copy.5.mask_ref
  0.8 0.8 copy.4.pat_ref
  1.5 0.0 copy-start
  1.5 1.1 copy-done
  2.7 147.5 %gather_and_multiply.1 = f32[1536,384]{1,0:T(8,128)S(1)} custom-call(bf16[2,1536,128]{2,1,0:T(8,128)(2,1)S(1)} %copy-done, s32[2,12,1]{2,1,0:T(8,128)S(1)} %copy.4.pat_ref, s32[12,3]{1,0:T(8,128)S(1)} %copy.5.mask_ref), custom_call_target="tpu_custom_call" | custom-call | flops 9663676416 | bytes 2359296 | tf_op jit(solution)/shard_map/gather_and_multiply/pallas_call | solution.py:362
  150.2 1.4 copy.7
Async XLA Ops:
  1.5 1.1 copy-start

commit v3 on v2

v3 whole, which is shorter than its diff:
```python
import functools

import jax
import jax.numpy as jnp
from jax import lax
from jax.experimental import pallas as pl
from jax.experimental.pallas import tpu as pltpu
from jax.sharding import PartitionSpec as P

TILE = 128
SECTIONS = 2
MESH = pl.DeviceIdType.MESH
START_Y = 2
EARLY_SCATTER, SCATTER, PASS_ON = (1, 3), (3, 3), (2, 4)
CROSS = (4, 4, 4)
GATHER = (8, 9, 8)
FORWARD, FORWARD_ROOT, FORWARD_OPPOSITE = 10, 11, 10
FINAL = 13
RELIEVED = 2
LATE_Z = (7, 10, 13)
LAST_TICK = 26


def kernel(rows, a_ref, pat_ref, mask_ref, out_ref, row, col, acc, got, relay, transit,
           zs, zr, xs, xr, ys, cr, cs, rr, tr, es, er, ls):
    half, quarter = rows // 2, rows // 4
    width = half // 2
    tiles = rows // TILE

    row_id, col_id = lax.axis_index("row"), lax.axis_index("col")
    y, h = lax.div(row_id, 2), lax.rem(row_id, 2)
    x, zl, core = lax.div(col_id, 8), lax.rem(lax.div(col_id, 2), 4), lax.rem(col_id, 2)
    a, b = lax.div(zl, 2), lax.rem(zl, 2)
    x_up, x_down, x_far = lax.rem(x + 1, 4), lax.rem(x + 3, 4), lax.rem(x + 2, 4)
    ring = lax.rem(y - x + 4, 4)
    straight = h == a

    def device(x=x, y=y, h=h, zl=zl, core=core):
        return (y * 2 + h, x * 8 + zl * 2 + core)

    dev_x_up, dev_x_down = device(x=x_up), device(x=x_down)
    dev_y_up, dev_y_down = device(y=lax.rem(y + 1, 4)), device(y=lax.rem(y + 3, 4))
    dev_over, dev_core = device(h=1 - h, zl=2 * (1 - a) + b), device(core=1 - core)
    z_peers = [2 * lax.rem(a + k // 2, 2) + lax.rem(b + k % 2, 2) for k in (1, 2, 3)]
    partners = [dev_x_up, dev_x_down, dev_y_up, dev_y_down, dev_over, dev_core]
    partners += [device(zl=z) for z in z_peers]

    barrier = pltpu.get_barrier_semaphore()
    for partner in partners:
        pl.semaphore_signal(barrier, inc=1, device_id=partner, device_id_type=MESH)

    own = x * 4 + zl

    load = pltpu.make_async_copy(a_ref, row.at[own], ls)
    load.start()
    load.wait()

    def mask_tile(t, _):
        place = pl.ds(pl.multiple_of(t * TILE, TILE), TILE)
        for section in range(SECTIONS):
            keep = pat_ref[section, 0, t].astype(jnp.float32)
            tile = row[own, section, place, :].astype(jnp.float32) * keep
            row[own, section, place, :] = tile.astype(jnp.bfloat16)
        return 0

    lax.fori_loop(0, tiles, mask_tile, 0)
    pl.semaphore_wait(barrier, len(partners))

    def send(src, dst, send_sem, recv_sem, target):
        return pltpu.make_async_remote_copy(
            src_ref=src, dst_ref=dst, send_sem=send_sem, recv_sem=recv_sem,
            device_id=target, device_id_type=MESH)

    def row_half(s, g):
        return row.at[s, :, pl.ds(pl.multiple_of(g * half, half), half), :]

    def row_part(s, g, q):
        return row.at[s, :, pl.ds(pl.multiple_of(g * half + q * quarter, quarter), quarter), :]

    def col_part(s, q):
        return col.at[s, :, pl.ds(pl.multiple_of(q * quarter, quarter), quarter), :]

    def z_of(k, first=a):
        return 2 * lax.rem(first + lax.div(k, 2), 2) + lax.rem(b + lax.rem(k, 2), 2)

    def item(i):
        k = lax.rem(i, 4)
        return k, z_of(k), lax.rem(b + lax.div(i, 4), 2)

    def wait_row(s, g, q):
        ref = row_part(s, g, q)
        send(ref, ref, xs.at[0, 0, 0], xr.at[s, g, q], dev_x_up).wait_recv()

    def wait_col(s, q):
        ref = col_part(s, q)
        send(ref, ref, xs.at[0, 0, 0], cr.at[s, q], dev_y_up).wait_recv()

    def send_item(i):
        _, z, g = item(i)
        s = x * 4 + z
        for n, (way, q, target) in enumerate(
                ((0, 0, dev_x_up), (1, 1, dev_x_down), (0, 1, dev_x_up), (1, 0, dev_x_down))):
            ref = row_part(s, g, q)
            send(ref, ref, xs.at[way, i, n // 2], xr.at[s, g, q], target).start()

    send_item(jnp.int32(0))
    def send_along_z(late, n):
        g = lax.rem(z_peers[n] + late, 2)
        ref = row_half(own, g)
        send(ref, ref, zs.at[late, n], zr.at[zl, g], device(zl=z_peers[n])).start()

    for n in range(3):
        send_along_z(0, n)
    acc[...] = jnp.zeros_like(acc)

    def slice_of(n, first=h):
        o = lax.rem(n, 4)
        step = jnp.where(o == 0, 0, jnp.where(o == 1, 3, jnp.where(o == 2, 1, 2)))
        return lax.rem(x + step, 4) * 4 + z_of(lax.div(n, 4), first)

    def crossing(j, r, first=h):
        o = jnp.where(r == 0, 3, jnp.where(r == 2, 0, lax.div(r + 1, 2)))
        return slice_of(4 * j + o, first)

    def accumulate(group, f):
        place = pl.ds(pl.multiple_of(lax.rem(b + f, 2) * half, half), half)
        slices = [slice_of(group * 4 + o) for o in range(4)]
        left = jnp.concatenate([row[s, e, place, :] for s in slices for e in range(SECTIONS)], axis=1)
        right = jnp.concatenate([col[s, e] for s in slices for e in range(SECTIONS)], axis=1)
        total = lax.dot_general(left, right, (((1,), (1,)), ((), ())), preferred_element_type=jnp.float32)
        for side in range(2):
            acc[side, place, :] += total[:, side * width:(side + 1) * width]

    def tick(m, _):
        i, sub = lax.div(m, 3), lax.rem(m, 3)

        @pl.when((sub == 0) & (i >= 1) & (i <= 8))
        def _():
            _, z, g = item(i - 1)
            wait_row(x_down * 4 + z, g, 1)
            wait_row(x_up * 4 + z, g, 0)
            wait_row(x_far * 4 + z, g, 0)
            wait_row(x_far * 4 + z, g, 1)

        @pl.when((sub == 1) & (i < 8))
        def _():
            _, z, g = item(i)
            for way, q, source, target in ((0, 0, x_down, dev_x_up), (1, 1, x_up, dev_x_down)):
                s = source * 4 + z
                wait_row(s, g, q)
                ref = row_part(s, g, q)
                send(ref, ref, xs.at[way, i, 2], xr.at[s, g, q], target).start()

        @pl.when((sub == 2) & (i < 7))
        def _():
            k, z, g = item(i + 1)

            @pl.when(k != 0)
            def _():
                ref = row_half(x * 4 + z, g)
                send(ref, ref, xs.at[0, 0, 0], zr.at[z, g], dev_x_up).wait_recv()

            send_item(i + 1)

        for n in range(3):
            @pl.when(m == LATE_Z[n])
            def _():
                send_along_z(1, n)

        @pl.when(straight)
        def _():
            @pl.when((ring == 0) & (m >= START_Y) & (m < START_Y + 16))
            def _():
                s = slice_of(m - START_Y)
                col[s] = row[s, :, pl.ds(pl.multiple_of(b * half, half), half), :]
                for q, target in ((0, dev_y_up), (1, dev_y_down)):
                    send(row_part(s, b, q), col_part(s, q), ys.at[q, m - START_Y, 0], cr.at[s, q], target).start()

            for q, target in ((0, dev_y_up), (1, dev_y_down)):
                hops = ring if q == 0 else 4 - ring
                n = m - START_Y - 2 * hops

                @pl.when((ring != 0) & (n >= 0) & (n < 16))
                def _():
                    s = slice_of(n)
                    wait_col(s, q)

                    @pl.when(hops < 3)
                    def _():
                        ref = col_part(s, q)
                        send(ref, ref, ys.at[q, n, 0], cr.at[s, q], target).start()

        @pl.when(jnp.logical_not(straight))
        def _():
            def at(when):
                first, step = when if isinstance(when, tuple) else (when, 4)
                since = m - first + 4 * step
                here = (m >= first) & (m < first + 4 * step) & (lax.rem(since, step) == 0)
                return here, lax.div(since, step) - 4

            def by_place(ticks):
                return jnp.where(ring == 0, ticks[0], jnp.where(ring == 2, ticks[2], ticks[1]))

            r_down, r_up, r_far = lax.rem(ring + 3, 4), lax.rem(ring + 1, 4), lax.rem(ring + 2, 4)
            beside = lax.rem(ring, 2) == 1

            def scatter(j, jobs):
                for n, r, q, dst, recv_sem, target in jobs:
                    send(row_part(crossing(j, r, a), b, q), dst, cs.at[j, n], recv_sem, target).start()

            here, j = at(EARLY_SCATTER)

            @pl.when((ring == 0) & here)
            def _():
                scatter(j, ((0, 2, 0, transit.at[j], tr.at[j], dev_y_up),
                            (1, 2, 1, transit.at[j], tr.at[j], dev_y_down)))

            here, j = at(SCATTER)

            @pl.when((ring == 0) & here)
            def _():
                jobs = []
                for q in range(2):
                    jobs.append((2 + q, 1, q, relay.at[j, q], rr.at[j, q], dev_y_up))
                    jobs.append((4 + q, 3, q, relay.at[j, q], rr.at[j, q], dev_y_down))
                s = crossing(j, 0, a)
                for q in range(2):
                    jobs.append((6 + q, 0, q, col_part(s, q), cr.at[s, q], dev_over))
                scatter(j, jobs)

            here, j = at(PASS_ON)

            @pl.when(beside & here)
            def _():
                send(transit.at[j], transit.at[j], cs.at[j, 0], tr.at[j], dev_y_up).wait_recv()

                @pl.when(ring == 1)
                def _():
                    send(transit.at[j], relay.at[j, 0], cs.at[j, 0], rr.at[j, 0], dev_y_up).start()

                @pl.when(ring == 3)
                def _():
                    send(transit.at[j], relay.at[j, 1], cs.at[j, 0], rr.at[j, 1], dev_y_down).start()

            here, j = at(by_place(CROSS))

            @pl.when((ring != 0) & here)
            def _():
                s = crossing(j, ring, a)
                for q in range(2):
                    ref = relay.at[j, q]
                    send(ref, ref, cs.at[j, 6 + q], rr.at[j, q], dev_over).wait_recv()
                    send(ref, col_part(s, q), cs.at[j, 6 + q], cr.at[s, q], dev_over).start()

            here, j = at(by_place(GATHER))

            @pl.when(here)
            def _():
                s = crossing(j, ring)
                for q in range(2):
                    wait_col(s, q)
                for n, (way, q, target) in enumerate(
                        ((0, 0, dev_y_up), (1, 1, dev_y_down), (0, 1, dev_y_up), (1, 0, dev_y_down))):
                    ref = col_part(s, q)
                    send(ref, ref, ys.at[way, j, n // 2], cr.at[s, q], target).start()

            for way, r, target in ((0, r_down, dev_y_up), (1, r_up, dev_y_down)):
                here, j = at(jnp.where(beside, jnp.where(r == 0, FORWARD_ROOT, FORWARD_OPPOSITE), FORWARD))

                @pl.when(here)
                def _():
                    s = crossing(j, r)
                    wait_col(s, way)

                    @pl.when((ring != 0) | (j >= RELIEVED))
                    def _():
                        ref = col_part(s, way)
                        send(ref, ref, ys.at[way, j, 2], cr.at[s, way], target).start()

                    @pl.when((ring == 2) & (j < RELIEVED))
                    def _():
                        wait_col(s, 1 - way)
                        ref = col_part(s, 1 - way)
                        send(ref, ref, ys.at[way, j, 3], cr.at[s, 1 - way], target).start()

            here, j = at(FINAL)

            @pl.when(here)
            def _():
                @pl.when((ring != 2) | (j >= RELIEVED))
                def _():
                    for way, r in ((0, r_down), (1, r_up)):
                        wait_col(crossing(j, r), 1 - way)

                for q in range(2):
                    wait_col(crossing(j, r_far), q)

        start = jnp.where(straight, 12, FINAL + 1)
        first_due = (m >= start) & (m < start + 12) & (lax.rem(m + 16 - start, 4) == 0)
        second_due = jnp.where(straight, (m >= 15) & (m < 24) & (sub == 0), (m == 21) | (m == 23) | (m == 24))
        second = jnp.where(straight, i - 5, jnp.where(m == 21, 0, jnp.where(m == 23, 2, 1)))

        def product(f, _):
            @pl.when(jnp.where(f == 0, first_due, second_due))
            def _():
                accumulate(jnp.where(f == 0, lax.div(m + 16 - start, 4) - 4, second), f)
            return 0

        lax.fori_loop(0, 2, product, 0)
        return 0

    lax.fori_loop(0, LAST_TICK, tick, 0)

    def trade(f):
        g = lax.rem(b + f, 2)
        place = pl.ds(pl.multiple_of(g * half, half), half)
        return send(acc.at[1 - core, place, :], got.at[place, :], es.at[f], er.at[f], dev_core)

    def last(f, _):
        accumulate(3, f)
        trade(f).start()
        return 0

    lax.fori_loop(0, 2, last, 0)

    def settle(f, _):
        trade(f).wait_recv()
        first = lax.rem(b + f, 2) * (tiles // 2)

        def finish(t, _):
            tile_row = first + t
            place = pl.ds(pl.multiple_of(tile_row * TILE, TILE), TILE)
            for c in range(width // TILE):
                span = pl.ds(c * TILE, TILE)
                keep = mask_ref[c, tile_row].astype(jnp.float32)
                out_ref[place, span] = (acc[core, place, span] + got[place, span]) * keep
            return 0

        lax.fori_loop(0, tiles // 2, finish, 0)
        trade(f).wait_send()
        return 0

    lax.fori_loop(0, 2, settle, 0)

    part = row_part(0, 0, 0)
    whole = row_half(0, 0)
    for late in range(2):
        for n in range(3):
            send(whole, whole, zs.at[late, n], zr.at[0, 0], dev_x_up).wait_send()

    def drain_x(i, _):
        for way in range(2):
            for n in range(3):
                send(part, part, xs.at[way, i, n], xr.at[0, 0, 0], dev_x_up).wait_send()
        return 0

    lax.fori_loop(0, 8, drain_x, 0)

    @pl.when(straight)
    def _():
        def drain(n, _):
            for q in range(2):
                hops = ring if q == 0 else lax.rem(4 - ring, 4)

                @pl.when(hops < 3)
                def _():
                    send(part, part, ys.at[q, n, 0], xr.at[0, 0, 0], dev_x_up).wait_send()
            return 0

        lax.fori_loop(0, 16, drain, 0)

    @pl.when(jnp.logical_not(straight))
    def _():
        def drain(j, _):
            for way in range(2):
                for n in range(4):
                    done = (n < 2) | ((n == 2) & ((ring != 0) | (j >= RELIEVED)))

                    @pl.when(done | ((n == 3) & (ring == 2) & (j < RELIEVED)))
                    def _():
                        send(part, part, ys.at[way, j, n], xr.at[0, 0, 0], dev_x_up).wait_send()
            for n in range(8):
                @pl.when((ring == 0) | (n >= 6) | ((n == 0) & (ring != 2)))
                def _():
                    send(part, part, cs.at[j, n], xr.at[0, 0, 0], dev_x_up).wait_send()
            return 0

        lax.fori_loop(0, 4, drain, 0)


def shards(a_values, a_pattern, c_mask):
    rows, depth = a_values.shape[1], a_values.shape[2]
    out_width = c_mask.shape[1] * TILE
    half = rows // 2
    vmem = pl.BlockSpec(memory_space=pltpu.VMEM)
    smem = pl.BlockSpec(memory_space=pltpu.SMEM)
    dma = pltpu.SemaphoreType.DMA
    return pl.pallas_call(
        functools.partial(kernel, rows),
        out_shape=jax.ShapeDtypeStruct((rows, out_width), jnp.float32),
        in_specs=[pl.BlockSpec(memory_space=pl.ANY), smem, smem],
        out_specs=vmem,
        scratch_shapes=[
            pltpu.VMEM((16, SECTIONS, rows, depth), jnp.bfloat16),
            pltpu.VMEM((16, SECTIONS, half, depth), jnp.bfloat16),
            pltpu.VMEM((2, rows, out_width), jnp.float32),
            pltpu.VMEM((rows, out_width), jnp.float32),
            pltpu.VMEM((4, 2, SECTIONS, half // 2, depth), jnp.bfloat16),
            pltpu.VMEM((4, SECTIONS, half // 2, depth), jnp.bfloat16),
            dma((2, 3)), dma((4, 2)), dma((2, 8, 3)), dma((16, 2, 2)),
            dma((2, 16, 4)), dma((16, 2)), dma((4, 8)), dma((4, 2)), dma((4,)), dma((2,)), dma((2,)), dma,
        ],
        compiler_params=pltpu.CompilerParams(
            collective_id=0, has_side_effects=True, vmem_limit_bytes=48 << 20),
        cost_estimate=pl.CostEstimate(
            flops=2 * rows * half * 16 * SECTIONS * depth, bytes_accessed=4 * rows * out_width, transcendentals=0),
        name="gather_and_multiply",
    )(a_values, a_pattern.transpose(0, 2, 1), c_mask.T)


def solution(mesh):
    return jax.shard_map(
        shards,
        mesh=mesh,
        in_specs=(P(None, "row", "col"), P(None, "row", "col"), P("row", "col")),
        out_specs=P("row", "col"),
        check_vma=False,
    )
```

time: 153 us -> 133 us (0.87)
  Pallas kernels: 148 us -> 128 us
    pallas_call x1, Pallas kernels: 148 us -> 128 us  [shards(): pl.pallas_call(functools.partial(kernel, rows), out_shape=jax.ShapeDtypeS...]
    unnamed x5 -> x7, local copies, waits for them, and re-layouts: 4.08 us -> 3.9 us
where the time goes in v3:
time: 133 us; the launch traced here: 132 us
  Pallas kernels  128 us (96%)
  local copies, waits for them, and re-layouts  3.9 us (3%)
    pallas_call x1, Pallas kernels, shards(): pl.pallas_call(functools.partial(kernel, rows), out_shape=jax.ShapeDtypeS...  128 us
    unnamed x7, local copies, waits for them, and re-layouts  3.9 us

profile of v3, /device:TPU:97, one launch (start us, length us, event | category | flops | bytes accessed | tf_op | source)
XLA Modules:
  0.0 131.7 jit_solution(10612005939820535702)
XLA Ops:
  0.0 0.0 copy-start
  0.0 1.1 copy-done
  1.1 0.0 copy-start.1
  1.1 0.7 copy-done.1
  1.8 0.0 copy-start.2
  1.8 0.7 copy-done.2
  2.5 127.7 %gather_and_multiply.1 = f32[1536,384]{1,0:T(8,128)S(1)} custom-call(bf16[2,1536,128]{2,1,0:T(8,128)(2,1)S(1)} %copy-done, s32[2,1,12]{2,1,0:T(1,128)S(1)} %bitcast.5, s32[3,12]{1,0:T(4,128)S(1)} %bitcast.4), custom_call_target="tpu_custom_call" | custom-call | flops 9663676416 | bytes 2359296 | tf_op jit(solution)/shard_map/gather_and_multiply/pallas_call | solution.py:398
  130.2 1.4 %copy.6 = f32[1536,384]{1,0:T(8,128)} copy(f32[1536,384]{1,0:T(8,128)S(1)} %gather_and_multiply.1) | data formatting | bytes 4718592
Async XLA Ops:
  0.0 1.1 copy-start
  1.1 0.7 copy-start.1
  1.8 0.7 copy-start.2

commit v4 on v3

--- a/solution.py
+++ b/solution.py
@@ -18,10 +18,10 @@
 FINAL = 13
 RELIEVED = 2
 LATE_Z = (7, 10, 13)
-LAST_TICK = 26
-
-
-def kernel(rows, a_ref, pat_ref, mask_ref, out_ref, row, col, acc, got, relay, transit,
+LAST_TICK = 24
+
+
+def kernel(rows, a_ref, pat_hbm, mask_hbm, out_ref, pat_ref, mask_ref, row, col, acc, got, relay, transit,
            zs, zr, xs, xr, ys, cr, cs, rr, tr, es, er, ls):
     half, quarter = rows // 2, rows // 4
     width = half // 2
@@ -51,9 +51,12 @@
 
     own = x * 4 + zl
 
-    load = pltpu.make_async_copy(a_ref, row.at[own], ls)
-    load.start()
-    load.wait()
+    loads = [pltpu.make_async_copy(src, dst, ls.at[n]) for n, (src, dst) in enumerate(
+        ((a_ref, row.at[own]), (pat_hbm, pat_ref), (mask_hbm, mask_ref)))]
+    for load in loads:
+        load.start()
+    for load in loads:
+        load.wait()
 
     def mask_tile(t, _):
         place = pl.ds(pl.multiple_of(t * TILE, TILE), TILE)
@@ -104,13 +107,17 @@
             send(ref, ref, xs.at[way, i, n // 2], xr.at[s, g, q], target).start()
 
     send_item(jnp.int32(0))
-    def send_along_z(late, n):
-        g = lax.rem(z_peers[n] + late, 2)
+    for n in range(3):
+        g = lax.rem(z_peers[n], 2)
         ref = row_half(own, g)
-        send(ref, ref, zs.at[late, n], zr.at[zl, g], device(zl=z_peers[n])).start()
-
-    for n in range(3):
-        send_along_z(0, n)
+        send(ref, ref, zs.at[0, n], zr.at[zl, g], device(zl=z_peers[n])).start()
+
+    def pass_along_z(k, way):
+        to = zl + 1 - 2 * way
+        block = 2 * lax.rem(lax.div(to + 4, 2) + k // 2, 2) + lax.rem(to + 4 + k % 2, 2)
+        due = (to >= 0) & (to < 4) & ((block <= zl) if way == 0 else (block >= zl))
+        ref = row_half(x * 4 + block, b)
+        return due, send(ref, ref, zs.at[1 + way, k - 1], zr.at[block, b], device(zl=lax.rem(to + 4, 4)))
     acc[...] = jnp.zeros_like(acc)
 
     def slice_of(n, first=h):
@@ -122,25 +129,44 @@
         o = jnp.where(r == 0, 3, jnp.where(r == 2, 0, lax.div(r + 1, 2)))
         return slice_of(4 * j + o, first)
 
-    def accumulate(group, f):
+    def accumulate(slices, f):
         place = pl.ds(pl.multiple_of(lax.rem(b + f, 2) * half, half), half)
-        slices = [slice_of(group * 4 + o) for o in range(4)]
         left = jnp.concatenate([row[s, e, place, :] for s in slices for e in range(SECTIONS)], axis=1)
         right = jnp.concatenate([col[s, e] for s in slices for e in range(SECTIONS)], axis=1)
         total = lax.dot_general(left, right, (((1,), (1,)), ((), ())), preferred_element_type=jnp.float32)
         for side in range(2):
             acc[side, place, :] += total[:, side * width:(side + 1) * width]
 
+    def group_slices(group):
+        return [slice_of(group * 4 + o) for o in range(4)]
+
+    r_down, r_up, r_far = lax.rem(ring + 3, 4), lax.rem(ring + 1, 4), lax.rem(ring + 2, 4)
+
+    def wait_near_rows(i):
+        _, z, g = item(i)
+        wait_row(x_down * 4 + z, g, 1)
+        wait_row(x_up * 4 + z, g, 0)
+
+    def wait_far_rows(i):
+        _, z, g = item(i)
+        wait_row(x_far * 4 + z, g, 0)
+        wait_row(x_far * 4 + z, g, 1)
+
+    def wait_near_columns(j):
+        for way, r in ((0, r_down), (1, r_up)):
+            wait_col(crossing(j, r), 1 - way)
+
+    def wait_far_columns(j):
+        for q in range(2):
+            wait_col(crossing(j, r_far), q)
+
     def tick(m, _):
         i, sub = lax.div(m, 3), lax.rem(m, 3)
 
-        @pl.when((sub == 0) & (i >= 1) & (i <= 8))
+        @pl.when((sub == 0) & (i >= 1))
         def _():
-            _, z, g = item(i - 1)
-            wait_row(x_down * 4 + z, g, 1)
-            wait_row(x_up * 4 + z, g, 0)
-            wait_row(x_far * 4 + z, g, 0)
-            wait_row(x_far * 4 + z, g, 1)
+            wait_near_rows(i - 1)
+            wait_far_rows(i - 1)
 
         @pl.when((sub == 1) & (i < 8))
         def _():
@@ -162,10 +188,13 @@
 
             send_item(i + 1)
 
-        for n in range(3):
-            @pl.when(m == LATE_Z[n])
-            def _():
-                send_along_z(1, n)
+        for k in (1, 2, 3):
+            for way in range(2):
+                due, one = pass_along_z(k, way)
+
+                @pl.when(due & (m == LATE_Z[k - 1]))
+                def _():
+                    one.start()
 
         @pl.when(straight)
         def _():
@@ -201,7 +230,6 @@
             def by_place(ticks):
                 return jnp.where(ring == 0, ticks[0], jnp.where(ring == 2, ticks[2], ticks[1]))
 
-            r_down, r_up, r_far = lax.rem(ring + 3, 4), lax.rem(ring + 1, 4), lax.rem(ring + 2, 4)
             beside = lax.rem(ring, 2) == 1
 
             def scatter(j, jobs):
@@ -289,21 +317,19 @@
             def _():
                 @pl.when((ring != 2) | (j >= RELIEVED))
                 def _():
-                    for way, r in ((0, r_down), (1, r_up)):
-                        wait_col(crossing(j, r), 1 - way)
-
-                for q in range(2):
-                    wait_col(crossing(j, r_far), q)
+                    wait_near_columns(j)
+
+                wait_far_columns(j)
 
         start = jnp.where(straight, 12, FINAL + 1)
         first_due = (m >= start) & (m < start + 12) & (lax.rem(m + 16 - start, 4) == 0)
-        second_due = jnp.where(straight, (m >= 15) & (m < 24) & (sub == 0), (m == 21) | (m == 23) | (m == 24))
-        second = jnp.where(straight, i - 5, jnp.where(m == 21, 0, jnp.where(m == 23, 2, 1)))
+        second_due = jnp.where(straight, (m >= 15) & (m < 24) & (sub == 0), (m == 21) | (m == 23))
+        second = jnp.where(straight, i - 5, jnp.where(m == 21, 0, 2))
 
         def product(f, _):
             @pl.when(jnp.where(f == 0, first_due, second_due))
             def _():
-                accumulate(jnp.where(f == 0, lax.div(m + 16 - start, 4) - 4, second), f)
+                accumulate(group_slices(jnp.where(f == 0, lax.div(m + 16 - start, 4) - 4, second)), f)
             return 0
 
         lax.fori_loop(0, 2, product, 0)
@@ -316,12 +342,46 @@
         place = pl.ds(pl.multiple_of(g * half, half), half)
         return send(acc.at[1 - core, place, :], got.at[place, :], es.at[f], er.at[f], dev_core)
 
+    @pl.when(jnp.logical_not(straight))
+    def _():
+        wait_near_rows(7)
+        wait_far_rows(7)
+
+    accumulate([jnp.where(straight, p, q) for p, q in zip(group_slices(3), group_slices(1))], jnp.where(straight, 0, 1))
+
+    @pl.when(straight)
+    def _():
+        trade(0).start()
+        wait_near_rows(7)
+
+    @pl.when(jnp.logical_not(straight))
+    def _():
+        wait_near_columns(3)
+
+    ends = [jnp.where(straight, slice_of(12 + o), crossing(3, lax.rem(ring + turn, 4)))
+            for o, turn in ((0, 0), (1, 3), (2, 1), (3, 2))]
+    first_half = jnp.where(straight, 1, 0)
+
+    def nearly(f, _):
+        accumulate(ends[:3], f)
+        return 0
+
+    lax.fori_loop(first_half, 2, nearly, 0)
+
+    @pl.when(straight)
+    def _():
+        wait_far_rows(7)
+
+    @pl.when(jnp.logical_not(straight))
+    def _():
+        wait_far_columns(3)
+
     def last(f, _):
-        accumulate(3, f)
+        accumulate(ends[3:], f)
         trade(f).start()
         return 0
 
-    lax.fori_loop(0, 2, last, 0)
+    lax.fori_loop(first_half, 2, last, 0)
 
     def settle(f, _):
         trade(f).wait_recv()
@@ -344,9 +404,14 @@
 
     part = row_part(0, 0, 0)
     whole = row_half(0, 0)
-    for late in range(2):
-        for n in range(3):
-            send(whole, whole, zs.at[late, n], zr.at[0, 0], dev_x_up).wait_send()
+    for n in range(3):
+        send(whole, whole, zs.at[0, n], zr.at[0, 0], dev_x_up).wait_send()
+        for way in range(2):
+            due, one = pass_along_z(n + 1, way)
+
+            @pl.when(due)
+            def _():
+                one.wait_send()
 
     def drain_x(i, _):
         for way in range(2):
@@ -393,22 +458,23 @@
     out_width = c_mask.shape[1] * TILE
     half = rows // 2
     vmem = pl.BlockSpec(memory_space=pltpu.VMEM)
-    smem = pl.BlockSpec(memory_space=pltpu.SMEM)
     dma = pltpu.SemaphoreType.DMA
     return pl.pallas_call(
         functools.partial(kernel, rows),
         out_shape=jax.ShapeDtypeStruct((rows, out_width), jnp.float32),
-        in_specs=[pl.BlockSpec(memory_space=pl.ANY), smem, smem],
+        in_specs=[pl.BlockSpec(memory_space=pl.ANY)] * 3,
         out_specs=vmem,
         scratch_shapes=[
+            pltpu.SMEM((SECTIONS, 1, rows // TILE), jnp.int32),
+            pltpu.SMEM((c_mask.shape[1], rows // TILE), jnp.int32),
             pltpu.VMEM((16, SECTIONS, rows, depth), jnp.bfloat16),
             pltpu.VMEM((16, SECTIONS, half, depth), jnp.bfloat16),
             pltpu.VMEM((2, rows, out_width), jnp.float32),
             pltpu.VMEM((rows, out_width), jnp.float32),
             pltpu.VMEM((4, 2, SECTIONS, half // 2, depth), jnp.bfloat16),
             pltpu.VMEM((4, SECTIONS, half // 2, depth), jnp.bfloat16),
-            dma((2, 3)), dma((4, 2)), dma((2, 8, 3)), dma((16, 2, 2)),
-            dma((2, 16, 4)), dma((16, 2)), dma((4, 8)), dma((4, 2)), dma((4,)), dma((2,)), dma((2,)), dma,
+            dma((3, 3)), dma((4, 2)), dma((2, 8, 3)), dma((16, 2, 2)),
+            dma((2, 16, 4)), dma((16, 2)), dma((4, 8)), dma((4, 2)), dma((4,)), dma((2,)), dma((2,)), dma((3,)),
         ],
         compiler_params=pltpu.CompilerParams(
             collective_id=0, has_side_effects=True, vmem_limit_bytes=48 << 20),

time: 133 us -> 132 us (level)
  no operation moved by 1% of the time
where the time goes in v4:
time: 132 us
  Pallas kernels  128 us (97%)
  local copies, waits for them, and re-layouts  3.9 us (3%)
    pallas_call x1, Pallas kernels, shards(): pl.pallas_call(functools.partial(kernel, rows), out_shape=jax.ShapeDtypeS...  128 us
    unnamed x7, local copies, waits for them, and re-layouts  3.9 us

profile of v4, /device:TPU:97, one launch (start us, length us, event | category | flops | bytes accessed | tf_op | source)
XLA Modules:
  0.0 131.6 jit_solution(2510121035764081457)
XLA Ops:
  0.0 0.0 copy-start
  0.0 1.1 copy-done
  1.1 0.0 copy-start.1
  1.1 0.7 copy-done.1
  1.8 0.0 copy-start.2
  1.8 0.7 copy-done.2
  2.5 127.7 %gather_and_multiply.1 = f32[1536,384]{1,0:T(8,128)S(1)} custom-call(bf16[2,1536,128]{2,1,0:T(8,128)(2,1)S(1)} %copy-done, s32[2,1,12]{2,1,0:T(1,128)S(1)} %bitcast.5, s32[3,12]{1,0:T(4,128)S(1)} %bitcast.4), custom_call_target="tpu_custom_call" | custom-call | flops 9663676416 | bytes 2359296 | tf_op jit(solution)/shard_map/gather_and_multiply/pallas_call | solution.py:462
  130.2 1.4 %copy.6 = f32[1536,384]{1,0:T(8,128)} copy(f32[1536,384]{1,0:T(8,128)S(1)} %gather_and_multiply.1) | data formatting | bytes 4718592
Async XLA Ops:
  0.0 1.1 copy-start
  1.1 0.7 copy-start.1
  1.8 0.7 copy-start.2

commit v5 on v4

--- a/solution.py
+++ b/solution.py
@@ -17,11 +17,12 @@
 FORWARD, FORWARD_ROOT, FORWARD_OPPOSITE = 10, 11, 10
 FINAL = 13
 RELIEVED = 2
-LATE_Z = (7, 10, 13)
+EARLY_Z = (0, 1)
+LATE_Z = (8, 11, 14)
 LAST_TICK = 24
 
 
-def kernel(rows, a_ref, pat_hbm, mask_hbm, out_ref, pat_ref, mask_ref, row, col, acc, got, relay, transit,
+def kernel(rows, a_ref, pat_hbm, mask_hbm, out_ref, pat_ref, mask_ref, row, col, acc, got, relay, transit, other_row, other_col,
            zs, zr, xs, xr, ys, cr, cs, rr, tr, es, er, ls):
     half, quarter = rows // 2, rows // 4
     width = half // 2
@@ -107,10 +108,12 @@
             send(ref, ref, xs.at[way, i, n // 2], xr.at[s, g, q], target).start()
 
     send_item(jnp.int32(0))
-    for n in range(3):
+    def send_along_z(n):
         g = lax.rem(z_peers[n], 2)
         ref = row_half(own, g)
         send(ref, ref, zs.at[0, n], zr.at[zl, g], device(zl=z_peers[n])).start()
+
+    send_along_z(0)
 
     def pass_along_z(k, way):
         to = zl + 1 - 2 * way
@@ -160,12 +163,30 @@
         for q in range(2):
             wait_col(crossing(j, r_far), q)
 
+    def scatter(j, jobs):
+        for n, r, q, dst, recv_sem, target in jobs:
+            send(row_part(crossing(j, r, a), b, q), dst, cs.at[j, n], recv_sem, target).start()
+
+    def scatter_near(j):
+        jobs = []
+        for q in range(2):
+            jobs.append((2 + q, 1, q, relay.at[j, q], rr.at[j, q], dev_y_up))
+            jobs.append((4 + q, 3, q, relay.at[j, q], rr.at[j, q], dev_y_down))
+        scatter(j, jobs)
+
+    scatters = jnp.logical_not(straight) & (ring == 0)
+
     def tick(m, _):
         i, sub = lax.div(m, 3), lax.rem(m, 3)
 
         @pl.when((sub == 0) & (i >= 1))
         def _():
             wait_near_rows(i - 1)
+
+            @pl.when(scatters & (i <= 4))
+            def _():
+                scatter_near(i - 1)
+
             wait_far_rows(i - 1)
 
         @pl.when((sub == 1) & (i < 8))
@@ -188,6 +209,11 @@
 
             send_item(i + 1)
 
+        for n in (1, 2):
+            @pl.when(m == EARLY_Z[n - 1])
+            def _():
+                send_along_z(n)
+
         for k in (1, 2, 3):
             for way in range(2):
                 due, one = pass_along_z(k, way)
@@ -232,10 +258,6 @@
 
             beside = lax.rem(ring, 2) == 1
 
-            def scatter(j, jobs):
-                for n, r, q, dst, recv_sem, target in jobs:
-                    send(row_part(crossing(j, r, a), b, q), dst, cs.at[j, n], recv_sem, target).start()
-
             here, j = at(EARLY_SCATTER)
 
             @pl.when((ring == 0) & here)
@@ -248,9 +270,6 @@
             @pl.when((ring == 0) & here)
             def _():
                 jobs = []
-                for q in range(2):
-                    jobs.append((2 + q, 1, q, relay.at[j, q], rr.at[j, q], dev_y_up))
-                    jobs.append((4 + q, 3, q, relay.at[j, q], rr.at[j, q], dev_y_down))
                 s = crossing(j, 0, a)
                 for q in range(2):
                     jobs.append((6 + q, 0, q, col_part(s, q), cr.at[s, q], dev_over))
@@ -347,6 +366,29 @@
         wait_near_rows(7)
         wait_far_rows(7)
 
+    ends = [jnp.where(straight, slice_of(12 + o), crossing(3, lax.rem(ring + turn, 4)))
+            for o, turn in ((0, 0), (1, 3), (2, 1), (3, 2))]
+    final = ends[3]
+
+    def half_place(f):
+        return pl.ds(pl.multiple_of(lax.rem(b + f, 2) * half, half), half)
+
+    def give_rows(f, n):
+        place = half_place(f)
+        return send(row.at[final, :, place, :], other_row.at[:, place, :], es.at[n], er.at[n], dev_core)
+
+    def give_columns(n):
+        return send(col.at[final], other_col, es.at[n], er.at[n], dev_core)
+
+    @pl.when(straight)
+    def _():
+        give_columns(2).start()
+
+    @pl.when(jnp.logical_not(straight))
+    def _():
+        give_rows(0, 2).start()
+        give_rows(1, 3).start()
+
     accumulate([jnp.where(straight, p, q) for p, q in zip(group_slices(3), group_slices(1))], jnp.where(straight, 0, 1))
 
     @pl.when(straight)
@@ -358,12 +400,11 @@
     def _():
         wait_near_columns(3)
 
-    ends = [jnp.where(straight, slice_of(12 + o), crossing(3, lax.rem(ring + turn, 4)))
-            for o, turn in ((0, 0), (1, 3), (2, 1), (3, 2))]
     first_half = jnp.where(straight, 1, 0)
 
     def nearly(f, _):
         accumulate(ends[:3], f)
+        trade(f).start()
         return 0
 
     lax.fori_loop(first_half, 2, nearly, 0)
@@ -371,14 +412,27 @@
     @pl.when(straight)
     def _():
         wait_far_rows(7)
+        give_rows(1, 4).start()
+        give_columns(2).wait_recv()
+        give_rows(1, 4).wait_recv()
 
     @pl.when(jnp.logical_not(straight))
     def _():
         wait_far_columns(3)
+        give_columns(4).start()
+        give_rows(0, 2).wait_recv()
+        give_rows(1, 3).wait_recv()
+        give_columns(4).wait_recv()
 
     def last(f, _):
-        accumulate(ends[3:], f)
-        trade(f).start()
+        place = half_place(f)
+        span = pl.ds(pl.multiple_of(core * width, width), width)
+        left = jnp.concatenate([row[final, e, place, :] for e in range(SECTIONS)]
+                               + [other_row[e, place, :] for e in range(SECTIONS)], axis=1)
+        right = jnp.concatenate([col[final, e, span, :] for e in range(SECTIONS)]
+                                + [other_col[e, span, :] for e in range(SECTIONS)], axis=1)
+        acc[core, place, :] += lax.dot_general(
+            left, right, (((1,), (1,)), ((), ())), preferred_element_type=jnp.float32)
         return 0
 
     lax.fori_loop(first_half, 2, last, 0)
@@ -401,6 +455,17 @@
         return 0
 
     lax.fori_loop(0, 2, settle, 0)
+
+    @pl.when(straight)
+    def _():
+        give_columns(2).wait_send()
+        give_rows(1, 4).wait_send()
+
+    @pl.when(jnp.logical_not(straight))
+    def _():
+        give_rows(0, 2).wait_send()
+        give_rows(1, 3).wait_send()
+        give_columns(4).wait_send()
 
     part = row_part(0, 0, 0)
     whole = row_half(0, 0)
@@ -473,8 +538,10 @@
             pltpu.VMEM((rows, out_width), jnp.float32),
             pltpu.VMEM((4, 2, SECTIONS, half // 2, depth), jnp.bfloat16),
             pltpu.VMEM((4, SECTIONS, half // 2, depth), jnp.bfloat16),
+            pltpu.VMEM((SECTIONS, rows, depth), jnp.bfloat16),
+            pltpu.VMEM((SECTIONS, half, depth), jnp.bfloat16),
             dma((3, 3)), dma((4, 2)), dma((2, 8, 3)), dma((16, 2, 2)),
-            dma((2, 16, 4)), dma((16, 2)), dma((4, 8)), dma((4, 2)), dma((4,)), dma((2,)), dma((2,)), dma((3,)),
+            dma((2, 16, 4)), dma((16, 2)), dma((4, 8)), dma((4, 2)), dma((4,)), dma((5,)), dma((5,)), dma((3,)),
         ],
         compiler_params=pltpu.CompilerParams(
             collective_id=0, has_side_effects=True, vmem_limit_bytes=48 << 20),

time: 132 us -> 130 us (0.985)
  Pallas kernels: 128 us -> 126 us
    pallas_call x1, Pallas kernels: 128 us -> 126 us  [shards(): pl.pallas_call(functools.partial(kernel, rows), out_shape=jax.ShapeDtypeS...]
where the time goes in v5:
time: 130 us
  Pallas kernels  126 us (97%)
  local copies, waits for them, and re-layouts  3.9 us (3%)
    pallas_call x1, Pallas kernels, shards(): pl.pallas_call(functools.partial(kernel, rows), out_shape=jax.ShapeDtypeS...  126 us
    unnamed x7, local copies, waits for them, and re-layouts  3.9 us

profile of v5, /device:TPU:97, one launch (start us, length us, event | category | flops | bytes accessed | tf_op | source)
XLA Modules:
  0.0 130.2 jit_solution(14490885311548862584)
XLA Ops:
  0.0 0.0 copy-start
  0.0 1.1 copy-done
  1.1 0.0 copy-start.1
  1.1 0.7 copy-done.1
  1.8 0.0 copy-start.2
  1.8 0.7 copy-done.2
  2.5 126.3 %gather_and_multiply.1 = f32[1536,384]{1,0:T(8,128)S(1)} custom-call(bf16[2,1536,128]{2,1,0:T(8,128)(2,1)S(1)} %copy-done, s32[2,1,12]{2,1,0:T(1,128)S(1)} %bitcast.5, s32[3,12]{1,0:T(4,128)S(1)} %bitcast.4), custom_call_target="tpu_custom_call" | custom-call | flops 9663676416 | bytes 2359296 | tf_op jit(solution)/shard_map/gather_and_multiply/pallas_call | solution.py:527
  128.8 1.4 %copy.6 = f32[1536,384]{1,0:T(8,128)} copy(f32[1536,384]{1,0:T(8,128)S(1)} %gather_and_multiply.1) | data formatting | bytes 4718592
Async XLA Ops:
  0.0 1.1 copy-start
  1.1 0.7 copy-start.1
  1.8 0.7 copy-start.2

commit v6 on v5

--- a/solution.py
+++ b/solution.py
@@ -52,22 +52,28 @@
 
     own = x * 4 + zl
 
-    loads = [pltpu.make_async_copy(src, dst, ls.at[n]) for n, (src, dst) in enumerate(
-        ((a_ref, row.at[own]), (pat_hbm, pat_ref), (mask_hbm, mask_ref)))]
+    def own_half(g):
+        return pl.ds(pl.multiple_of(g * half, half), half)
+
+    loads = [pltpu.make_async_copy(pat_hbm, pat_ref, ls.at[0])]
+    for n in range(2):
+        place = own_half(lax.rem(b + n, 2))
+        loads.append(pltpu.make_async_copy(a_ref.at[:, place, :], row.at[own, :, place, :], ls.at[1 + n]))
+    loads.append(pltpu.make_async_copy(mask_hbm, mask_ref, ls.at[3]))
     for load in loads:
         load.start()
-    for load in loads:
-        load.wait()
-
-    def mask_tile(t, _):
-        place = pl.ds(pl.multiple_of(t * TILE, TILE), TILE)
-        for section in range(SECTIONS):
-            keep = pat_ref[section, 0, t].astype(jnp.float32)
-            tile = row[own, section, place, :].astype(jnp.float32) * keep
-            row[own, section, place, :] = tile.astype(jnp.bfloat16)
-        return 0
-
-    lax.fori_loop(0, tiles, mask_tile, 0)
+
+    def mask_half(g):
+        for t in range(tiles // 2):
+            place = pl.ds(pl.multiple_of(g * half + t * TILE, TILE), TILE)
+            for section in range(SECTIONS):
+                keep = pat_ref[section, 0, g * (tiles // 2) + t].astype(jnp.float32)
+                tile = row[own, section, place, :].astype(jnp.float32) * keep
+                row[own, section, place, :] = tile.astype(jnp.bfloat16)
+
+    loads[0].wait()
+    loads[1].wait()
+    mask_half(b)
     pl.semaphore_wait(barrier, len(partners))
 
     def send(src, dst, send_sem, recv_sem, target):
@@ -108,6 +114,10 @@
             send(ref, ref, xs.at[way, i, n // 2], xr.at[s, g, q], target).start()
 
     send_item(jnp.int32(0))
+    loads[2].wait()
+    mask_half(1 - b)
+    loads[3].wait()
+
     def send_along_z(n):
         g = lax.rem(z_peers[n], 2)
         ref = row_half(own, g)
@@ -541,7 +551,7 @@
             pltpu.VMEM((SECTIONS, rows, depth), jnp.bfloat16),
             pltpu.VMEM((SECTIONS, half, depth), jnp.bfloat16),
             dma((3, 3)), dma((4, 2)), dma((2, 8, 3)), dma((16, 2, 2)),
-            dma((2, 16, 4)), dma((16, 2)), dma((4, 8)), dma((4, 2)), dma((4,)), dma((5,)), dma((5,)), dma((3,)),
+            dma((2, 16, 4)), dma((16, 2)), dma((4, 8)), dma((4, 2)), dma((4,)), dma((5,)), dma((5,)), dma((4,)),
         ],
         compiler_params=pltpu.CompilerParams(
             collective_id=0, has_side_effects=True, vmem_limit_bytes=48 << 20),

time: 130 us -> 130 us (level)
  no operation moved by 1% of the time
where the time goes in v6:
time: 130 us
  Pallas kernels  126 us (97%)
  local copies, waits for them, and re-layouts  3.9 us (3%)
    pallas_call x1, Pallas kernels, shards(): pl.pallas_call(functools.partial(kernel, rows), out_shape=jax.ShapeDtypeS...  126 us
    unnamed x7, local copies, waits for them, and re-layouts  3.9 us

profile of v6, /device:TPU:97, one launch (start us, length us, event | category | flops | bytes accessed | tf_op | source)
XLA Modules:
  0.0 130.3 jit_solution(2409044283874766953)
XLA Ops:
  0.0 0.0 copy-start
  0.0 1.1 copy-done
  1.1 0.0 copy-start.1
  1.1 0.7 copy-done.1
  1.8 0.0 copy-start.2
  1.8 0.7 copy-done.2
  2.5 126.4 %gather_and_multiply.1 = f32[1536,384]{1,0:T(8,128)S(1)} custom-call(bf16[2,1536,128]{2,1,0:T(8,128)(2,1)S(1)} %copy-done, s32[2,1,12]{2,1,0:T(1,128)S(1)} %bitcast.5, s32[3,12]{1,0:T(4,128)S(1)} %bitcast.4), custom_call_target="tpu_custom_call" | custom-call | flops 9663676416 | bytes 2359296 | tf_op jit(solution)/shard_map/gather_and_multiply/pallas_call | solution.py:537
  128.9 1.4 %copy.6 = f32[1536,384]{1,0:T(8,128)} copy(f32[1536,384]{1,0:T(8,128)S(1)} %gather_and_multiply.1) | data formatting | bytes 4718592
Async XLA Ops:
  0.0 1.1 copy-start
  1.1 0.7 copy-start.1
  1.8 0.7 copy-start.2

commit v7 on v6

--- a/solution.py
+++ b/solution.py
@@ -197,7 +197,9 @@
             def _():
                 scatter_near(i - 1)
 
-            wait_far_rows(i - 1)
+            @pl.when(scatters | (i > 4))
+            def _():
+                wait_far_rows(i - 1)
 
         @pl.when((sub == 1) & (i < 8))
         def _():
@@ -207,6 +209,10 @@
                 wait_row(s, g, q)
                 ref = row_part(s, g, q)
                 send(ref, ref, xs.at[way, i, 2], xr.at[s, g, q], target).start()
+
+            @pl.when(jnp.logical_not(scatters) & (i >= 1) & (i <= 4))
+            def _():
+                wait_far_rows(i - 1)
 
         @pl.when((sub == 2) & (i < 7))
         def _():

time: 130 us -> 131 us (level)
  no operation moved by 1% of the time
where the time goes in v7:
time: 131 us
  Pallas kernels  127 us (97%)
  local copies, waits for them, and re-layouts  3.9 us (3%)
    pallas_call x1, Pallas kernels, shards(): pl.pallas_call(functools.partial(kernel, rows), out_shape=jax.ShapeDtypeS...  127 us
    unnamed x7, local copies, waits for them, and re-layouts  3.9 us

profile of v7, /device:TPU:97, one launch (start us, length us, event | category | flops | bytes accessed | tf_op | source)
XLA Modules:
  0.0 130.7 jit_solution(3650131947441840780)
XLA Ops:
  0.0 0.0 copy-start
  0.0 1.1 copy-done
  1.1 0.0 copy-start.1
  1.1 0.7 copy-done.1
  1.8 0.0 copy-start.2
  1.8 0.7 copy-done.2
  2.5 126.8 %gather_and_multiply.1 = f32[1536,384]{1,0:T(8,128)S(1)} custom-call(bf16[2,1536,128]{2,1,0:T(8,128)(2,1)S(1)} %copy-done, s32[2,1,12]{2,1,0:T(1,128)S(1)} %bitcast.5, s32[3,12]{1,0:T(4,128)S(1)} %bitcast.4), custom_call_target="tpu_custom_call" | custom-call | flops 9663676416 | bytes 2359296 | tf_op jit(solution)/shard_map/gather_and_multiply/pallas_call | solution.py:543
  129.3 1.4 %copy.6 = f32[1536,384]{1,0:T(8,128)} copy(f32[1536,384]{1,0:T(8,128)S(1)} %gather_and_multiply.1) | data formatting | bytes 4718592
Async XLA Ops:
  0.0 1.1 copy-start
  1.1 0.7 copy-start.1
  1.8 0.7 copy-start.2
